TPU v7x, 32 devices: a whole 2x2x4 slice. The times are simulated.
32 devices in a mesh: lon: 8 (over y, x, core), lat: 4 (over z).
Axes of the slice: x: 2, y: 2, z: 4, core: 2. Of those that a mesh axis runs over, the one named last changes fastest.
Arguments:
- cells: bfloat16 [256, 512, 128], P('lat', 'lon'), may hold values from -6 to 6
- ocean_mask: int32 [256, 512], P('lat', 'lon'), may hold values from 0 to 1, as said below
- cotangent: bfloat16 [256, 512, 128], P('lat', 'lon'), may hold values from -6 to 6
- kernel: float32 [7, 7, 128], replicated, may hold values from -0.875 to 0.875
- conv_bias: float32 [128], replicated, may hold values from -3 to 3
- gain: float32 [128], replicated, may hold values from 0.1 to 1.9
- shift: float32 [128], replicated, may hold values from -3 to 3
- w_in: bfloat16 [128, 512], replicated, may hold values from -0.5 to 0.5
- b_in: float32 [512], replicated, may hold values from -3 to 3
- w_out: bfloat16 [512, 128], replicated, may hold values from -0.25 to 0.25
Outputs:
- cells_grad: bfloat16 [256, 512, 128], P('lat', 'lon')
- grad_kernel: float32 [7, 7, 128], replicated
- grad_bias: float32 [128], replicated
- grad_gain: float32 [128], replicated
- grad_shift: float32 [128], replicated
- grad_in: float32 [128, 512], replicated
- grad_b: float32 [512], replicated
- grad_out: float32 [512, 128], replicated
Inputs may be any that keep to these rules, and one draw needn't show every extreme that they name: `ocean_mask`: within each aligned 64 x 64 block the ocean cells are either all cells, none, or those on one side of a straight line; some blocks are all land and some all ocean.
All inputs are finite; a program needn't handle non-finite values.
Results may differ from a plain program's by a relative error of at most 0.006.
Values may be sent and summed in bfloat16 or wider, within the bound.
A program may use at most 128 MiB of HBM per device.

v0:
```python
import jax
import jax.numpy as jnp
from jax import lax
from jax.sharding import PartitionSpec as P

KS = 7
HALF = 3


def with_halo(block, sides, width, periodic):
    for axis, dim in sides:
        count = lax.axis_size(axis)
        forward = [(i, i + 1) for i in range(count - 1)]
        if periodic:
            forward.append((count - 1, 0))
        backward = [(target, source) for source, target in forward]
        low = lax.ppermute(
            lax.slice_in_dim(block, block.shape[dim] - width, None, axis=dim), axis, forward
        )
        high = lax.ppermute(lax.slice_in_dim(block, 0, width, axis=dim), axis, backward)
        block = jnp.concatenate([low, block, high], axis=dim)
    return block


def depthwise(padded, kernel, height, across):
    summed = jnp.zeros((height, across, padded.shape[2]), jnp.float32)
    for row_off in range(KS):
        for col_off in range(KS):
            summed = summed + kernel[row_off, col_off] * padded[
                row_off : row_off + height, col_off : col_off + across
            ].astype(jnp.float32)
    return summed


def transposed(padded, kernel, height, across):
    summed = jnp.zeros((height, across, padded.shape[2]), jnp.float32)
    for row_off in range(KS):
        for col_off in range(KS):
            first_row = KS - 1 - row_off
            first_col = KS - 1 - col_off
            summed = summed + kernel[row_off, col_off] * padded[
                first_row : first_row + height, first_col : first_col + across
            ].astype(jnp.float32)
    return summed


def gelu_tanh(value):
    return jax.nn.gelu(value, approximate=True)


def section_one(padded, out_grad, cycle, kernel, conv_bias, gain, shift, w_in, b_in, w_out):
    ext_h, ext_w, channels = out_grad.shape
    height = ext_h - 2 * cycle
    across = ext_w - 2 * cycle
    conv = depthwise(padded, kernel, ext_h, ext_w) + conv_bias
    average = jnp.mean(conv, axis=-1, keepdims=True)
    centred = conv - average
    variance = jnp.mean(centred * centred, axis=-1, keepdims=True)
    inverse_std = lax.rsqrt(variance + 1e-06)
    scaled = centred * inverse_std
    normed = (scaled * gain + shift).astype(jnp.bfloat16).reshape(ext_h * ext_w, channels)
    preact = jnp.dot(normed, w_in, preferred_element_type=jnp.float32) + b_in
    activation = gelu_tanh(preact).astype(jnp.bfloat16)
    flat_grad = out_grad.reshape(ext_h * ext_w, channels)
    act_grad = lax.dot_general(
        flat_grad, w_out, (((1,), (1,)), ((), ())), preferred_element_type=jnp.float32
    )
    hidden_grad = jax.vjp(gelu_tanh, preact)[1](act_grad)[0].astype(jnp.bfloat16)
    inner_act = activation.reshape(ext_h, ext_w, -1).reshape(height * across, -1)
    inner_grad = out_grad.reshape(height * across, channels)
    grad_out = lax.dot_general(
        inner_act, inner_grad, (((0,), (0,)), ((), ())), preferred_element_type=jnp.float32
    )
    return (normed, scaled, inverse_std, hidden_grad, grad_out)


def section_two(padded, normed, scaled, inverse_std, hidden_grad, cycle, gain, w_in):
    ext_h, ext_w, channels = scaled.shape
    height = ext_h - 2 * cycle
    across = ext_w - 2 * cycle
    norm_grad = lax.dot_general(
        hidden_grad, w_in, (((1,), (1,)), ((), ())), preferred_element_type=jnp.float32
    ).reshape(ext_h, ext_w, channels)
    weighted = norm_grad * gain
    conv_grad = (
        inverse_std
        * (
            weighted
            - jnp.mean(weighted, axis=-1, keepdims=True)
            - scaled * jnp.mean(weighted * scaled, axis=-1, keepdims=True)
        )
    ).astype(jnp.bfloat16)
    hidden_in = hidden_grad.reshape(ext_h, ext_w, -1).reshape(height * across, -1)
    normed_in = normed.reshape(ext_h, ext_w, channels).reshape(height * across, channels)
    grad_in = lax.dot_general(
        normed_in, hidden_in, (((0,), (0,)), ((), ())), preferred_element_type=jnp.float32
    )
    grad_b = jnp.sum(hidden_in.astype(jnp.float32), axis=0)
    grad_gain = jnp.sum(norm_grad * scaled, axis=(0, 1))
    grad_shift = jnp.sum(norm_grad, axis=(0, 1))
    conv_wide = conv_grad.astype(jnp.float32)
    grad_bias = jnp.sum(conv_wide, axis=(0, 1))
    rows_list = []
    for row_off in range(KS):
        cols_list = []
        for col_off in range(KS):
            window = padded[row_off : row_off + height, col_off : col_off + across].astype(
                jnp.float32
            )
            cols_list.append(jnp.sum(conv_wide * window, axis=(0, 1)))
        rows_list.append(jnp.stack(cols_list))
    grad_kernel = jnp.stack(rows_list)
    return (conv_grad, grad_kernel, grad_bias, grad_gain, grad_shift, grad_in, grad_b)


def body(cells, ocean_mask, cotangent, kernel, conv_bias, gain, shift, w_in, b_in, w_out):
    height, across, channels = cells.shape
    ocean = ocean_mask.astype(jnp.bfloat16)[..., None]
    masked = cells * ocean
    out_grad = cotangent * ocean
    widened = with_halo(masked, (("lon", 1),), HALF, True)
    padded = with_halo(widened, (("lat", 0),), HALF, False)
    cycle = 0
    normed, scaled, inverse_std, hidden_grad, grad_out = section_one(
        padded, out_grad, cycle, kernel, conv_bias, gain, shift, w_in, b_in, w_out
    )
    conv_grad, grad_kernel, grad_bias, grad_gain, grad_shift, grad_in, grad_b = section_two(
        padded, normed, scaled, inverse_std, hidden_grad, cycle, gain, w_in
    )
    wide_grad = with_halo(conv_grad, (("lon", 1),), HALF, True)
    grad_padded = with_halo(wide_grad, (("lat", 0),), HALF, False)
    grad_kernel, grad_bias, grad_gain, grad_shift, grad_in, grad_b, grad_out = lax.psum(
        (grad_kernel, grad_bias, grad_gain, grad_shift, grad_in, grad_b, grad_out), ("lon", "lat")
    )
    spread_back = transposed(grad_padded, kernel, height, across)
    cells_grad = ((cotangent.astype(jnp.float32) + spread_back) * ocean.astype(jnp.float32)).astype(
        jnp.bfloat16
    )
    factor = lax.rsqrt(jnp.float32(height * across * lax.axis_size("lon") * lax.axis_size("lat")))
    return (
        cells_grad,
        grad_kernel * factor,
        grad_bias * factor,
        grad_gain * factor,
        grad_shift * factor,
        grad_in * factor,
        grad_b * factor,
        grad_out * factor,
    )


def solution(mesh):
    in_specs = (
        P("lat", "lon", None),
        P("lat", "lon"),
        P("lat", "lon", None),
        P(),
        P(),
        P(),
        P(),
        P(),
        P(),
        P(),
    )
    out_specs = (P("lat", "lon", None), P(), P(), P(), P(), P(), P(), P())
    return jax.shard_map(body, mesh=mesh, in_specs=in_specs, out_specs=out_specs, check_vma=False)
```

profile of v0, /device:TPU:0, one launch (start us, length us, event | category | flops | bytes accessed | tf_op | source)
XLA Modules:
  0.0 273.0 jit_solution(1557221506595038402)
XLA Ops:
  7.2 0.8 fusion.144
  8.0 1.9 broadcast_multiply_fusion
  10.5 2.9 %collective-permute-start.1 = (bf16[64,3,128]{2,1,0:T(4,128)(2,1)S(1)}, bf16[64,3,128]{2,1,0:T(4,128)(2,1)S(1)}, u32[]{:S(2)}, u32[]{:S(2)}) collective-permute-start(bf16[64,3,128]{2,1,0:T(4,128)(2,1)S(1)} %get-tuple-element.95), channel_id=1, source_target_pairs={{4,0},{8,4},{12,8},{16,12},{20,16},{24,20},{28,24},{0,28},{5,1},{9... | collective-permute-start | bytes 147464 | tf_op jit(solution)/shard_map/ppermute | solution.py:20
  13.5 1.9 collective-permute-done
  15.4 4.2 %collective-permute-start.2 = (bf16[3,70,128]{2,1,0:T(8,128)(2,1)S(1)}, bf16[3,70,128]{2,1,0:T(8,128)(2,1)S(1)}, u32[]{:S(2)}, u32[]{:S(2)}) collective-permute-start(bf16[3,70,128]{2,1,0:T(8,128)(2,1)S(1)} %get-tuple-element.90), channel_id=1, source_target_pairs={{0,1},{1,2},{2,3},{4,5},{5,6},{6,7},{8,9},{9,10},{10,11},{12,13},{... | collective-permute-start | bytes 161288 | tf_op jit(solution)/shard_map/ppermute | solution.py:17
  19.7 1.3 collective-permute-start.3
  21.6 4.1 %collective-permute-done.3 = bf16[3,70,128]{2,1,0:T(8,128)(2,1)S(1)} collective-permute-done((bf16[3,70,128]{2,1,0:T(8,128)(2,1)S(1)}, bf16[3,70,128]{2,1,0:T(8,128)(2,1)S(1)}, u32[]{:S(2)}, u32[]{:S(2)}) %collective-permute-start.3) | collective-permute-done | bytes 53792 | tf_op jit(solution)/shard_map/ppermute | solution.py:20
  26.4 16.3 %fusion.145 = (f32[64,64]{1,0:T(8,128)S(1)}, f32[64,64,128]{2,1,0:T(8,128)S(1)}) fusion(f32[128]{0:T(128)S(1)} %copy-done.11, bf16[67,70,128]{2,1,0:T(8,128)(2,1)S(1)} %get-tuple-element.89, f32[128]{0:T(128)S(1)} %get-tuple-element.143, f32[128]{0:T(128)S(1)} %get-tuple-element.144, f32[128]{0:T(128)S(1)} %get-tuple-element.97, ...), kind=kLoop, calls=%fused_computation.356 | loop fusion | flops 87027712 | bytes 47326208 | tf_op jit(solution)/shard_map/reduce_sum | solution.py:56
  42.7 1.3 multiply_reduce_fusion.3
  44.0 1.3 add_convert_fusion
  45.3 1.2 fusion.149
  46.6 4.2 %fusion.7 = f32[512,128]{1,0:T(8,128)} fusion(bf16[4096,128]{1,0:T(8,128)(2,1)S(1)} %bitcast.179, f32[4096,512]{1,0:T(8,128)S(1)} %fusion.149, f32[512]{0:T(512)S(1)} %copy-done.14), kind=kOutput, calls=%fused_computation.62 | convolution fusion | flops 557842432 | bytes 9701376 | tf_op jit(solution)/shard_map/dot_general | solution.py:71
  50.8 6.7 %convert_reduce_fusion.1 = (f32[512]{0:T(512)S(1)}, bf16[4096,512]{1,0:T(8,128)(2,1)S(1)}) fusion(f32[4096,512]{1,0:T(8,128)S(1)} %fusion.149, f32[512]{0:T(512)S(1)} %copy-done.14, bf16[4096,128]{1,0:T(8,128)(2,1)S(1)} %bitcast.180, bf16[512,128]{1,0:T(8,128)(2,1)S(1)} %copy-done.13), kind=kOutput, calls=%fused_computation.61 | convolution fusion | flops 585104896 | bytes 13766656 | tf_op jit(solution)/shard_map/dot_general | solution.py:65
  57.5 1.9 copy-done.7
  59.4 1.5 fusion.150
  60.8 4.8 %fusion.143 = (f32[128]{0:T(128)S(1)}, f32[4096]{0:T(1024)S(1)}, f32[4096,128]{1,0:T(8,128)}) fusion(f32[128]{0:T(128)S(1)} %copy-done.10, bf16[4096,512]{1,0:T(8,128)(2,1)} %copy-done.7, bf16[128,512]{1,0:T(8,128)(2,1)S(1)} %copy-done), kind=kOutput, calls=%fused_computation.354 | convolution fusion | flops 538439552 | bytes 6439936 | tf_op jit(solution)/shard_map/dot_general | solution.py:81
  65.7 4.6 %multiply_reduce_fusion = (f32[128]{0:T(128)S(1)}, f32[64,64]{1,0:T(8,128)S(1)}) fusion(f32[64,64,128]{2,1,0:T(8,128)} %copy-done.3, f32[64,64]{1,0:T(8,128)S(1)} %add_rsqrt_fusion, f32[64,64]{1,0:T(8,128)S(1)} %broadcast_multiply_fusion.5, f32[4096,128]{1,0:T(8,128)} %get-tuple-element.147, f32[64,64,128]{2,1,0:T(8,128)} %bitcast.176, f32[128]{0:T(128)S(1)} %copy-done.10), kind=kLoop, calls=%fused_computation.234 | loop fusion | flops 3665792 | bytes 6341632 | tf_op jit(solution)/shard_map/reduce_sum | solution.py:99
  70.3 6.4 %fusion.129 = (f32[128]{0:T(128)S(1)}, f32[128]{0:T(128)S(1)}, f32[128]{0:T(128)S(1)}, f32[128]{0:T(128)S(1)}, f32[128]{0:T(128)S(1)}, /*index=5*/f32[128]{0:T(1...) fusion(bf16[67,70,128]{2,1,0:T(8,128)(2,1)S(1)} %get-tuple-elem, ...), kind=kLoop, calls=%fused_computation.233 | loop fusion | flops 33027840 | bytes 24192512 | tf_op jit(solution)/shard_map/reduce_sum | solution.py:110
  76.8 0.9 fusion.84
  77.7 5.3 %fusion.101 = (f32[128]{0:T(128)S(1)}, f32[128]{0:T(128)S(1)}, f32[128]{0:T(128)S(1)}, f32[128]{0:T(128)S(1)}, f32[128]{0:T(128)S(1)}, /*index=5*/f32[128]{0:T(1...) fusion(bf16[64,64,128]{2,1,0:T(8,128)(2,1)S(1)} %get-tuple-elem, ...), kind=kLoop, calls=%fused_computation.205 | loop fusion | flops 29357696 | bytes 19932672 | tf_op jit(solution)/shard_map/reduce_sum | solution.py:110
  83.2 8.6 %fusion.128 = (f32[128]{0:T(128)S(1)}, f32[128]{0:T(128)S(1)}, f32[128]{0:T(128)S(1)}, f32[128]{0:T(128)S(1)}, f32[128]{0:T(128)S(1)}, /*index=5*/f32[128]{0:T(1...) fusion(bf16[64,64,128]{2,1,0:T(8,128)(2,1)} %copy-done.1, ...), kind=kLoop, calls=%fused_computation.232 | loop fusion | flops 25688832 | bytes 5346304 | tf_op jit(solution)/shard_map/reduce_sum | solution.py:110
  91.9 40.2 %all-reduce = (f32[7,7,128]{2,1,0:T(8,128)S(1)}, f32[128]{0:T(128)S(1)}, f32[128]{0:T(128)S(1)}, f32[128]{0:T(128)S(1)}, f32[512]{0:T(512)S(1)}) all-reduce(f32[7,7,128]{2,1,0:T(8,128)S(1)} %constant_dynamic-update-slice_fusion, f32[128]{0:T(128)S(1)} %get-tuple-element.64, ...), channel_id=1, replica_groups=mesh['lon'=8,'lat'=4] {'lon','lat'}, use_global_device_ids=true, to_apply=%region_53.0 | all-reduce | flops 7168 | bytes 57344 | tf_op jit(solution)/shard_map/psum | solution.py:132
  133.4 1.0 collective-permute-start.5
  134.9 1.4 collective-permute-done.5
  136.3 2.9 %collective-permute-done.4 = bf16[64,3,128]{2,1,0:T(4,128)(2,1)S(1)} collective-permute-done((bf16[64,3,128]{2,1,0:T(4,128)(2,1)S(1)}, bf16[64,3,128]{2,1,0:T(4,128)(2,1)S(1)}, u32[]{:S(2)}, u32[]{:S(2)}) %collective-permute-start.4) | collective-permute-done | bytes 49184 | tf_op jit(solution)/shard_map/ppermute | solution.py:17
  139.3 1.4 collective-permute-start.6
  140.7 4.5 %collective-permute-start.7 = (bf16[3,70,128]{2,1,0:T(8,128)(2,1)S(1)}, bf16[3,70,128]{2,1,0:T(8,128)(2,1)S(1)}, u32[]{:S(2)}, u32[]{:S(2)}) collective-permute-start(bf16[3,70,128]{2,1,0:T(8,128)(2,1)S(1)} %get-tuple-element.87), channel_id=1, source_target_pairs={{0,1},{1,2},{2,3},{4,5},{5,6},{6,7},{8,9},{9,10},{10,11},{12,13},{... | collective-permute-start | bytes 161288 | tf_op jit(solution)/shard_map/ppermute | solution.py:17
  145.8 1.3 collective-permute-done.7
  147.7 16.7 %multiply_convert_fusion.2 = bf16[64,64,128]{2,1,0:T(8,128)(2,1)} fusion(bf16[64,64,128]{2,1,0:T(8,128)(2,1)S(1)} %copy-done.8, bf16[64,64,128]{2,1,0:T(8,128)(2,1)S(1)} %copy-done.2, bf16[64,3,128]{2,1,0:T(4,128)(2,1)S(1)} %collective-permute-done.4, bf16[64,3,128]{2,1,0:T(4,128)(2,1)S(1)} %collective-permute-done.5, ...), kind=kLoop, calls=%fused_computation.235 | loop fusion | flops 88080384 | bytes 47325696 | tf_op jit(solution)/shard_map/convert_element_type | solution.py:136
  164.3 98.5 %all-reduce.4.cloned.1.call-done = (f32[128,512]{1,0:T(8,128)}, f32[512,128]{1,0:T(8,128)}) async-done(((f32[128,512]{1,0:T(8,128)}, f32[512,128]{1,0:T(8,128)}), (f32[128,512]{1,0:T(8,128)}, f32[512,128]{1,0:T(8,128)})) %all-reduce.4.cloned.1.call-update) | async-done | bytes 524304 | tf_op jit(solution)/shard_map/psum | solution.py:132
  262.8 1.7 broadcast_multiply_fusion.3
  264.5 1.7 broadcast_multiply_fusion.2
  (68 shorter events, 5.3 us)
Async XLA Ops:
  7.2 38.2 %copy-start = (bf16[128,512]{1,0:T(8,128)(2,1)S(1)}, bf16[128,512]{1,0:T(8,128)(2,1)}, u32[]{:S(2)}) copy-start(bf16[128,512]{1,0:T(8,128)(2,1)} %param.17) | copy-start | bytes 393220
  7.2 255.6 %all-reduce.4.cloned.1.call-start = ((), (), s32[]{:S(2)}) async-start(), calls=%async_computation | async-start | bytes 1048576 | tf_op jit(solution)/shard_map/psum | solution.py:132
  8.0 5.5 %copy-start.9 = (f32[7,7,128]{2,1,0:T(8,128)S(1)}, f32[7,7,128]{2,1,0:T(8,128)}, u32[]{:S(2)}) copy-start(f32[7,7,128]{2,1,0:T(8,128)} %param.13) | copy-start | bytes 75268
  10.0 16.4 %copy-start.6 = (bf16[64,64,128]{2,1,0:T(8,128)(2,1)}, bf16[64,64,128]{2,1,0:T(8,128)(2,1)S(1)}, u32[]{:S(2)}) copy-start(bf16[64,64,128]{2,1,0:T(8,128)(2,1)S(1)} %get-tuple-element.146) | copy-start | bytes 3145732
  10.0 5.3 %collective-permute-start = (bf16[64,3,128]{2,1,0:T(4,128)(2,1)S(1)}, bf16[64,3,128]{2,1,0:T(4,128)(2,1)S(1)}, u32[]{:S(2)}, u32[]{:S(2)}) collective-permute-start(bf16[64,3,128]{2,1,0:T(4,128)(2,1)S(1)} %get-tuple-element.94), channel_id=1, source_target_pairs={{0,4},{4,8},{8,12},{12,16},{16,20},{20,24},{24,28},{28,0},{1,5},{5... | collective-permute-start | bytes 147464 | tf_op jit(solution)/shard_map/ppermute | solution.py:17
  10.5 4.9 %collective-permute-start.1 = (bf16[64,3,128]{2,1,0:T(4,128)(2,1)S(1)}, bf16[64,3,128]{2,1,0:T(4,128)(2,1)S(1)}, u32[]{:S(2)}, u32[]{:S(2)}) collective-permute-start(bf16[64,3,128]{2,1,0:T(4,128)(2,1)S(1)} %get-tuple-element.95), channel_id=1, source_target_pairs={{4,0},{8,4},{12,8},{16,12},{20,16},{24,20},{28,24},{0,28},{5,1},{9... | collective-permute-start | bytes 147464 | tf_op jit(solution)/shard_map/ppermute | solution.py:20
  15.4 10.9 %copy-start.11 = (f32[128]{0:T(128)S(1)}, f32[128]{0:T(128)}, u32[]{:S(2)}) copy-start(f32[128]{0:T(128)} %param.14) | copy-start | bytes 1540
  15.4 6.2 %collective-permute-start.2 = (bf16[3,70,128]{2,1,0:T(8,128)(2,1)S(1)}, bf16[3,70,128]{2,1,0:T(8,128)(2,1)S(1)}, u32[]{:S(2)}, u32[]{:S(2)}) collective-permute-start(bf16[3,70,128]{2,1,0:T(8,128)(2,1)S(1)} %get-tuple-element.90), channel_id=1, source_target_pairs={{0,1},{1,2},{2,3},{4,5},{5,6},{6,7},{8,9},{9,10},{10,11},{12,13},{... | collective-permute-start | bytes 161288 | tf_op jit(solution)/shard_map/ppermute | solution.py:17
  19.7 6.1 %collective-permute-start.3 = (bf16[3,70,128]{2,1,0:T(8,128)(2,1)S(1)}, bf16[3,70,128]{2,1,0:T(8,128)(2,1)S(1)}, u32[]{:S(2)}, u32[]{:S(2)}) collective-permute-start(bf16[3,70,128]{2,1,0:T(8,128)(2,1)S(1)} %get-tuple-element.91), channel_id=1, source_target_pairs={{1,0},{2,1},{3,2},{5,4},{6,5},{7,6},{9,8},{10,9},{11,10},{13,12},{... | collective-permute-start | bytes 161288 | tf_op jit(solution)/shard_map/ppermute | solution.py:20
  42.7 2.6 copy-start.3
  42.7 1.4 copy-start.10
  42.7 1.4 copy-start.12
  45.3 1.3 copy-start.14
  46.6 4.2 %copy-start.13 = (bf16[512,128]{1,0:T(8,128)(2,1)S(1)}, bf16[512,128]{1,0:T(8,128)(2,1)}, u32[]{:S(2)}) copy-start(bf16[512,128]{1,0:T(8,128)(2,1)} %param.19) | copy-start | bytes 393220
  57.4 1.9 copy-start.7
  65.7 4.6 %copy-start.4 = (f32[64,64,128]{2,1,0:T(8,128)S(1)}, f32[64,64,128]{2,1,0:T(8,128)}, u32[]{:S(2)}) copy-start(f32[64,64,128]{2,1,0:T(8,128)} %copy-done.3) | copy-start | bytes 6291460
  65.7 4.6 %copy-start.5 = (f32[4096,128]{1,0:T(8,128)S(1)}, f32[4096,128]{1,0:T(8,128)}, u32[]{:S(2)}) copy-start(f32[4096,128]{1,0:T(8,128)} %get-tuple-element.147) | copy-start | bytes 6291460
  76.8 6.2 %copy-start.1 = (bf16[64,64,128]{2,1,0:T(8,128)(2,1)}, bf16[64,64,128]{2,1,0:T(8,128)(2,1)S(1)}, u32[]{:S(2)}) copy-start(bf16[64,64,128]{2,1,0:T(8,128)(2,1)S(1)} %get-tuple-element.79) | copy-start | bytes 3145732
  83.2 56.0 %copy-start.2 = (bf16[64,64,128]{2,1,0:T(8,128)(2,1)S(1)}, bf16[64,64,128]{2,1,0:T(8,128)(2,1)}, u32[]{:S(2)}) copy-start(bf16[64,64,128]{2,1,0:T(8,128)(2,1)} %copy-done.1) | copy-start | bytes 3145732
  133.4 2.9 %collective-permute-start.5 = (bf16[64,3,128]{2,1,0:T(4,128)(2,1)S(1)}, bf16[64,3,128]{2,1,0:T(4,128)(2,1)S(1)}, u32[]{:S(2)}, u32[]{:S(2)}) collective-permute-start(bf16[64,3,128]{2,1,0:T(4,128)(2,1)S(1)} %get-tuple-element.92), channel_id=1, source_target_pairs={{4,0},{8,4},{12,8},{16,12},{20,16},{24,20},{28,24},{0,28},{5,1},{9... | collective-permute-start | bytes 147464 | tf_op jit(solution)/shard_map/ppermute | solution.py:20
  134.3 4.9 %collective-permute-start.4 = (bf16[64,3,128]{2,1,0:T(4,128)(2,1)S(1)}, bf16[64,3,128]{2,1,0:T(4,128)(2,1)S(1)}, u32[]{:S(2)}, u32[]{:S(2)}) collective-permute-start(bf16[64,3,128]{2,1,0:T(4,128)(2,1)S(1)} %get-tuple-element.93), channel_id=1, source_target_pairs={{0,4},{4,8},{8,12},{12,16},{16,20},{20,24},{24,28},{28,0},{1,5},{5... | collective-permute-start | bytes 147464 | tf_op jit(solution)/shard_map/ppermute | solution.py:17
  139.2 8.4 %copy-start.8 = (bf16[64,64,128]{2,1,0:T(8,128)(2,1)S(1)}, bf16[64,64,128]{2,1,0:T(8,128)(2,1)}, u32[]{:S(2)}) copy-start(bf16[64,64,128]{2,1,0:T(8,128)(2,1)} %param.12) | copy-start | bytes 3145732
  139.3 6.5 %collective-permute-start.6 = (bf16[3,70,128]{2,1,0:T(8,128)(2,1)S(1)}, bf16[3,70,128]{2,1,0:T(8,128)(2,1)S(1)}, u32[]{:S(2)}, u32[]{:S(2)}) collective-permute-start(bf16[3,70,128]{2,1,0:T(8,128)(2,1)S(1)} %get-tuple-element.86), channel_id=1, source_target_pairs={{1,0},{2,1},{3,2},{5,4},{6,5},{7,6},{9,8},{10,9},{11,10},{13,12},{... | collective-permute-start | bytes 161288 | tf_op jit(solution)/shard_map/ppermute | solution.py:20
  140.7 6.3 %collective-permute-start.7 = (bf16[3,70,128]{2,1,0:T(8,128)(2,1)S(1)}, bf16[3,70,128]{2,1,0:T(8,128)(2,1)S(1)}, u32[]{:S(2)}, u32[]{:S(2)}) collective-permute-start(bf16[3,70,128]{2,1,0:T(8,128)(2,1)S(1)} %get-tuple-element.87), channel_id=1, source_target_pairs={{0,1},{1,2},{2,3},{4,5},{5,6},{6,7},{8,9},{9,10},{10,11},{12,13},{... | collective-permute-start | bytes 161288 | tf_op jit(solution)/shard_map/ppermute | solution.py:17
Sparse Core Ops, SparseCore 0:
  134.5 128.2 all-reduce.3
where the time goes:
time: 273 us
  waiting for transfers between devices  111 us (41%)
  other arithmetic  70.9 us (26%)
  blocking collectives  40.2 us (15%)
  matrix products  18.3 us (7%)
  starting transfers between devices  16 us (6%)
  between operations  14.4 us (5%)
    psum x1, waiting for transfers between devices, body(): lax.psum((grad_kernel, grad_bias, grad_gain, grad_shift, grad_in, grad_b,...  98.5 us
    psum x1, blocking collectives, body(): lax.psum((grad_kernel, grad_bias, grad_gain, grad_shift, grad_in, grad_b,...  40.2 us
    reduce_sum x4, other arithmetic, section_two(): cols_list.append(jnp.sum(conv_wide * window, axis=(0, 1)))  21.2 us
    convert_element_type x1, other arithmetic, body(): ((cotangent.astype(jnp.float32) + spread_back) * ocean.astype(jnp.float32...  16.7 us
    reduce_sum x1, other arithmetic, section_one(): average = jnp.mean(conv, axis=-1, keepdims=True)  16.3 us
    ppermute x4, starting transfers between devices, with_halo(): lax.ppermute(lax.slice_in_dim(block, block.shape[dim] - width, None, axis...  9.28 us
    ppermute x4, waiting for transfers between devices, with_halo(): lax.ppermute(lax.slice_in_dim(block, block.shape[dim] - width, None, axis...  6.73 us
    dot_general x1, matrix products, section_one(): lax.dot_general(flat_grad, w_out, (((1,), (1,)), ((), ())), preferred_ele...  6.66 us
  transfers between devices with their start and end apart: 9, of which 7 were waited for; matrix products, arithmetic and copies ran while one was open for 7% of the time, Pallas kernels for 0%

commit v1 on v0

v1 whole, which is shorter than its diff:
```python
import functools
import math

import jax
import jax.numpy as jnp
from jax import lax
from jax.experimental import pallas as pl
from jax.experimental.pallas import tpu as pltpu
from jax.sharding import PartitionSpec as P

KS = 7
HALF = 3
BS = 64
C = 128
HID = 512
LEFT = 8
WIDE = 80
TALL = BS + 2 * HALF
PAIRS = TALL // 2
BIG = 2 * HID
SMALL = 64
MESH = pl.DeviceIdType.MESH
F32 = jnp.float32
BF16 = jnp.bfloat16
MOVES = ((0, 1), (0, -1), (1, 0), (-1, 0), (1, 1), (1, -1), (-1, 1), (-1, -1))


def mm(a, b, dims=((1,), (0,))):
    return lax.dot_general(a, b, (dims, ((), ())), preferred_element_type=F32)


def plan(n_lon, n_lat):
    part = -(-BIG // (n_lon * n_lat * 16)) * 16
    small = max(SMALL // n_lon, 8)
    return part, small


def block_kernel(
    n_lon, n_lat,
    cells, mask, cot, kern, bias, gain, shift, w_in, b_in, w_out,
    o_cells, o_kernel, o_bias, o_gain, o_shift, o_in, o_b, o_out,
    padf, gradf, padp, gradp, w_fwd, w_bwd, convb, grad_t, maskx, acc_in, acc_out, vecs,
    h_send, h_recv, c_recv,
    big, big_lon, big_lat, big_sum, big_all, small, small_lon, small_lat, small_sum, small_all,
    hs_sem, hr_sem, s_sem, r_sem,
):
    part, small_part = plan(n_lon, n_lat)
    strip = n_lat * part
    lon = lax.axis_index("lon")
    lat = lax.axis_index("lat")
    lons = [lax.rem(lon + d, n_lon) for d in range(1, n_lon)]
    lats = [lax.rem(lat + d, n_lat) for d in range(1, n_lat)]

    def dev(a, b):
        return {"lat": a, "lon": b}

    def step_lon(d):
        return lax.rem(lon + d + n_lon, n_lon)

    def has(d):
        return (lat > 0) if d < 0 else (lat < n_lat - 1)

    barrier = pltpu.get_barrier_semaphore()
    for other in lons:
        pl.semaphore_signal(barrier, inc=1, device_id=dev(lat, other), device_id_type=MESH)
    for other in lats:
        pl.semaphore_signal(barrier, inc=1, device_id=dev(other, lon), device_id_type=MESH)
    for dlat, dlon in MOVES[4:]:
        corner = dev(lax.rem(lat + dlat + n_lat, n_lat), step_lon(dlon))
        pl.semaphore_signal(barrier, inc=1, device_id=corner, device_id_type=MESH)

    mask_t = mask[...].astype(F32).T
    padf3 = padf.reshape(TALL, WIDE, C)
    gradf3 = gradf.reshape(TALL, WIDE, C)
    for field in (padf3, gradf3):
        field[0:HALF] = jnp.zeros((HALF, WIDE, C), F32)
        field[BS + HALF : TALL] = jnp.zeros((HALF, WIDE, C), F32)
    for row in range(BS):
        spread = jnp.broadcast_to(mask_t[:, row : row + 1], (BS, C))
        maskx[row] = spread.astype(BF16)
        padf3[HALF + row, LEFT : LEFT + BS, :] = cells[row].astype(F32) * spread

    pl.semaphore_wait(barrier, n_lon + n_lat + 2)

    def halo_copy(turn, move):
        dlat, dlon = MOVES[move]
        if move < 4:
            src, dst = h_send.at[turn, move], h_recv.at[turn, move]
        else:
            src = h_send.at[turn, 2 if dlat > 0 else 3, :, pl.ds(48 if dlon > 0 else 0, 16), :]
            dst = c_recv.at[turn, move - 4]
        return pltpu.make_async_remote_copy(
            src_ref=src, dst_ref=dst,
            send_sem=hs_sem.at[turn, move], recv_sem=hr_sem.at[turn, move],
            device_id=dev(lat + dlat, step_lon(dlon)), device_id_type=MESH,
        )

    def halo_send(turn, field, field3):
        for k in range(HALF):
            last = field[pl.ds(HALF * WIDE + LEFT + BS - HALF + k, BS, stride=WIDE), :]
            first = field[pl.ds(HALF * WIDE + LEFT + k, BS, stride=WIDE), :]
            h_send[turn, 0, k] = last.astype(BF16)
            h_send[turn, 1, k] = first.astype(BF16)
            h_send[turn, 2, k] = field3[BS + k, LEFT : LEFT + BS, :].astype(BF16)
            h_send[turn, 3, k] = field3[HALF + k, LEFT : LEFT + BS, :].astype(BF16)
        for move, (dlat, _) in enumerate(MOVES):
            if dlat == 0:
                halo_copy(turn, move).start()
            else:
                @pl.when(has(dlat))
                def _(move=move):
                    halo_copy(turn, move).start()

    def halo_wait(turn, field, field3):
        for move, (dlat, dlon) in enumerate(MOVES):
            if dlat == 0:
                halo_copy(turn, move).wait()
                at = LEFT - HALF if dlon > 0 else LEFT + BS
                for k in range(HALF):
                    field[pl.ds(HALF * WIDE + at + k, BS, stride=WIDE), :] = h_recv[
                        turn, move, k
                    ].astype(F32)
            else:
                @pl.when(has(dlat))
                def _(move=move):
                    halo_copy(turn, move).wait_send()

                @pl.when(has(-dlat))
                def _(move=move, dlat=dlat, dlon=dlon):
                    halo_copy(turn, move).wait_recv()
                    at = 0 if dlat > 0 else BS + HALF
                    if move < 4:
                        field3[at : at + HALF, LEFT : LEFT + BS, :] = h_recv[turn, move].astype(F32)
                    else:
                        got = c_recv[turn, move - 4].astype(F32)
                        if dlon > 0:
                            field3[at : at + HALF, 0:LEFT, :] = got[:, 8:16, :]
                        else:
                            field3[at : at + HALF, LEFT + BS : WIDE, :] = got[:, 0:8, :]

    def spread_pairs(field3, pairs):
        def one(r, carry):
            for b in range(KS):
                for h in range(2):
                    pairs[b, r, :, h * C : (h + 1) * C] = field3[
                        2 * r + h, pl.ds(LEFT - HALF + b, BS), :
                    ].astype(BF16)
            return carry
        lax.fori_loop(0, PAIRS, one, 0)

    def conv_chunk(pairs, weights, t):
        taps = [
            pairs[b, pl.ds(8 * t + q, 8)].reshape(8 * BS, 2 * C) for b in range(KS) for q in range(4)
        ]
        return mm(jnp.concatenate(taps, axis=1), weights[...])

    halo_send(0, padf, padf3)

    eye = lax.broadcasted_iota(jnp.int32, (C, C), 0) == lax.broadcasted_iota(jnp.int32, (C, C), 1)
    none = jnp.zeros((C, C), BF16)
    for weights, flip in ((w_fwd, False), (w_bwd, True)):
        for b in range(KS):
            taps = []
            for a in range(KS):
                row = kern[KS - 1 - a, KS - 1 - b] if flip else kern[a, b]
                taps.append(jnp.where(eye, row[None, :], 0.0).astype(BF16))
            taps = [none] + taps + [none]
            for q in range(4):
                at = (b * 4 + q) * 2 * C
                weights[at : at + C, 0:C] = taps[2 * q + 1]
                weights[at : at + C, C : 2 * C] = taps[2 * q]
                weights[at + C : at + 2 * C, 0:C] = taps[2 * q + 2]
                weights[at + C : at + 2 * C, C : 2 * C] = taps[2 * q + 1]

    acc_in[...] = jnp.zeros_like(acc_in)
    acc_out[...] = jnp.zeros_like(acc_out)
    vecs[...] = jnp.zeros_like(vecs)
    halo_wait(0, padf, padf3)
    spread_pairs(padf3, padp)

    def forward(t, carry):
        convb[pl.ds(t * 512, 512), :] = conv_chunk(padp, w_fwd, t)
        return carry
    lax.fori_loop(0, 4, forward, 0)

    c1 = math.sqrt(2.0 / math.pi)
    c2 = c1 * 0.044715
    order = (0, 2, 4, 6, 1, 3, 5, 7)

    def cell_chunk(t, carry):
        two = convb[pl.ds(pl.multiple_of(t * 256, 256), 256), :]
        conv = jnp.concatenate([two[:, :C], two[:, C:]], axis=0) + bias[...]
        centred = conv - jnp.mean(conv, axis=-1, keepdims=True)
        inverse_std = lax.rsqrt(jnp.mean(centred * centred, axis=-1, keepdims=True) + 1e-06)
        scaled = centred * inverse_std
        normed = (scaled * gain[...] + shift[...]).astype(BF16)
        og = jnp.concatenate([cot[8 * t + i] * maskx[8 * t + i] for i in order], axis=0)
        normed_t = normed.T
        og_t = og.T
        ones = jnp.ones((16, 512), BF16)
        left = jnp.concatenate([normed_t, ones], axis=0)
        norm_grad = jnp.zeros((512, C), F32)
        for h in range(2):
            cols = slice(h * 256, (h + 1) * 256)
            v = mm(normed, w_in[:, cols]) + b_in[:, cols]
            act_grad = mm(og, w_out[cols, :], ((1,), (1,)))
            v2 = v * v
            t_half = 0.5 + 0.5 * jnp.tanh(v * (c1 + c2 * v2))
            act = v * t_half
            slope = t_half + act * (1.0 - t_half) * (2.0 * c1 + 6.0 * c2 * v2)
            hidden = (act_grad * slope).astype(BF16)
            acc_out[:, cols] += mm(og_t, act.astype(BF16))
            acc_in[:, cols] += mm(left, hidden)
            norm_grad += mm(hidden, w_in[:, cols], ((1,), (1,)))
        weighted = norm_grad * gain[...]
        product = norm_grad * scaled
        g = inverse_std * (
            weighted
            - jnp.mean(weighted, axis=-1, keepdims=True)
            - scaled * jnp.mean(weighted * scaled, axis=-1, keepdims=True)
        )
        g = g.astype(BF16)
        wide = g.astype(F32)
        vecs[0] += wide.reshape(64, 8, C).sum(0)
        vecs[1] += product.reshape(64, 8, C).sum(0)
        vecs[2] += norm_grad.reshape(64, 8, C).sum(0)
        grad_t[:, pl.ds(pl.multiple_of(t * 256, 256), 256)] = jnp.concatenate(
            [g[:256], g[256:]], axis=1
        ).T
        for n, i in enumerate(order):
            gradf3[HALF + 8 * t + i, LEFT : LEFT + BS, :] = wide[n * BS : (n + 1) * BS]
        return carry
    lax.fori_loop(0, 8, cell_chunk, 0)

    halo_send(1, gradf, gradf3)

    if big.shape[0] > BIG:
        big[BIG:, :] = jnp.zeros((big.shape[0] - BIG, C), F32)
    for h in range(4):
        big[h * C : (h + 1) * C, :] = acc_in[0:C, h * C : (h + 1) * C]
        big[HID + h * C : HID + (h + 1) * C, :] = acc_out[:, h * C : (h + 1) * C].T

    def copy(src, dst, group, mine, other, to):
        return pltpu.make_async_remote_copy(
            src_ref=src, dst_ref=dst.at[mine], send_sem=s_sem.at[group, other],
            recv_sem=r_sem.at[group, mine], device_id=to, device_id_type=MESH,
        )

    def arrived(dst, group, other, to):
        pltpu.make_async_remote_copy(
            src_ref=dst.at[other], dst_ref=dst.at[other], send_sem=s_sem.at[group, other],
            recv_sem=r_sem.at[group, other], device_id=to, device_id_type=MESH,
        ).wait_recv()

    def send_parts(src, rows, dst, group):
        for other in lons:
            at = pl.multiple_of(other * rows, 8)
            copy(src.at[pl.ds(at, rows)], dst, group, lon, other, dev(lat, other)).start()
        dst[lon] = src[pl.ds(pl.multiple_of(lon * rows, 8), rows), :]

    def end(src, rows, dst, group, peers, along):
        for other in peers:
            to = dev(lat, other) if along == "lon" else dev(other, lon)
            mine = lon if along == "lon" else lat
            copy(src.at[pl.ds(0, rows)], dst, group, mine, other, to).wait_send()
            arrived(dst, group, other, to)

    def total(slots, count):
        out = slots[0]
        for k in range(1, count):
            out = out + slots[k]
        return out

    send_parts(big, strip, big_lon, 0)

    def kernel_column(b, carry):
        rows = [jnp.zeros((1, C), F32) for _ in range(KS + 2)]
        for q in range(4):
            both = mm(grad_t[...], padp[b, q : q + 32].reshape(2048, 2 * C))

            def diagonal(e, s):
                block = both[e * C : (e + 1) * C, s * C : (s + 1) * C]
                return jnp.sum(jnp.where(eye, block, 0.0), axis=0, keepdims=True)
            rows[2 * q + 1] = rows[2 * q + 1] + diagonal(0, 0) + diagonal(1, 1)
            if q < 3:
                rows[2 * q + 2] = rows[2 * q + 2] + diagonal(0, 1)
            if q > 0:
                rows[2 * q] = rows[2 * q] + diagonal(1, 0)
        small[pl.ds(pl.multiple_of(b * 8, 8), 8), :] = jnp.concatenate(
            rows[1:8] + [jnp.zeros((1, C), F32)], axis=0
        )
        return carry
    lax.fori_loop(0, KS, kernel_column, 0)

    if small.shape[0] > SMALL:
        small[SMALL:, :] = jnp.zeros((small.shape[0] - SMALL, C), F32)
    small[56:64, :] = jnp.concatenate(
        [jnp.sum(vecs[k], axis=0, keepdims=True) for k in range(3)]
        + [acc_in[C : C + 1, h * C : (h + 1) * C] for h in range(4)]
        + [jnp.zeros((1, C), F32)],
        axis=0,
    )
    send_parts(small, small_part, small_lon, 1)

    halo_wait(1, gradf, gradf3)
    spread_pairs(gradf3, gradp)

    def backward(t):
        two = conv_chunk(gradp, w_bwd, t)
        for i in range(8):
            for e in range(2):
                row = 16 * t + 2 * i + e
                back = two[i * BS : (i + 1) * BS, e * C : (e + 1) * C]
                o_cells[row] = ((cot[row].astype(F32) + back) * maskx[row].astype(F32)).astype(BF16)

    backward(0)
    end(big, strip, big_lon, 0, lons, "lon")
    end(small, small_part, small_lon, 1, lons, "lon")
    big_sum[...] = total(big_lon, n_lon)
    small_sum[...] = total(small_lon, n_lon)
    for other in lats:
        at = pl.multiple_of(other * part, 8)
        copy(big_sum.at[pl.ds(at, part)], big_lat, 2, lat, other, dev(other, lon)).start()
        copy(small_sum, small_lat, 3, lat, other, dev(other, lon)).start()
    big_lat[lat] = big_sum[pl.ds(pl.multiple_of(lat * part, 8), part), :]
    small_lat[lat] = small_sum[...]

    backward(1)
    end(big_sum, part, big_lat, 2, lats, "lat")
    end(small_sum, small_part, small_lat, 3, lats, "lat")
    factor = 1.0 / math.sqrt(float(BS * BS * n_lon * n_lat))
    own = pl.ds(pl.multiple_of(lat * part, 8), part)
    big_all[lon, own, :] = total(big_lat, n_lat) * factor
    small_all[lon] = total(small_lat, n_lat) * factor

    def spread_lat(other):
        return pltpu.make_async_remote_copy(
            src_ref=big_all.at[lon, own], dst_ref=big_all.at[lon, own],
            send_sem=s_sem.at[4, other], recv_sem=r_sem.at[4, lat],
            device_id=dev(other, lon), device_id_type=MESH,
        )

    for other in lats:
        spread_lat(other).start()
    for other in lons:
        copy(small_all.at[lon], small_all, 6, lon, other, dev(lat, other)).start()

    backward(2)
    for other in lats:
        spread_lat(other).wait_send()
        theirs = big_all.at[lon, pl.ds(pl.multiple_of(other * part, 8), part)]
        pltpu.make_async_remote_copy(
            src_ref=theirs, dst_ref=theirs, send_sem=s_sem.at[4, other],
            recv_sem=r_sem.at[4, other], device_id=dev(other, lon), device_id_type=MESH,
        ).wait_recv()
    for other in lons:
        copy(big_all.at[lon], big_all, 5, lon, other, dev(lat, other)).start()

    backward(3)
    for other in lons:
        copy(big_all.at[lon], big_all, 5, lon, other, dev(lat, other)).wait_send()
        arrived(big_all, 5, other, dev(lat, other))
        copy(small_all.at[lon], small_all, 6, lon, other, dev(lat, other)).wait_send()
        arrived(small_all, 6, other, dev(lat, other))

    flat = big_all.reshape(n_lon * strip, C)
    for h in range(4):
        o_in[:, h * C : (h + 1) * C] = flat[h * C : (h + 1) * C, :]
    o_out[...] = flat[HID : 2 * HID, :]
    rest = small_all.reshape(n_lon * small_part, C)
    for a in range(KS):
        for b in range(KS):
            o_kernel[a, b : b + 1, :] = rest[8 * b + a : 8 * b + a + 1, :]
    o_bias[...] = rest[56:57, :]
    o_gain[...] = rest[57:58, :]
    o_shift[...] = rest[58:59, :]
    for h in range(4):
        o_b[:, h * C : (h + 1) * C] = rest[59 + h : 60 + h, :]


def body(n_lon, n_lat, cells, ocean_mask, cotangent, kernel, conv_bias, gain, shift, w_in, b_in, w_out):
    part, small_part = plan(n_lon, n_lat)
    strip = n_lat * part
    vmem = pl.BlockSpec(memory_space=pltpu.VMEM)
    most = max(n_lon, n_lat)
    outs = pl.pallas_call(
        functools.partial(block_kernel, n_lon, n_lat),
        out_shape=(
            jax.ShapeDtypeStruct((BS, BS, C), BF16),
            jax.ShapeDtypeStruct((KS, KS, C), F32),
            jax.ShapeDtypeStruct((1, C), F32),
            jax.ShapeDtypeStruct((1, C), F32),
            jax.ShapeDtypeStruct((1, C), F32),
            jax.ShapeDtypeStruct((C, HID), F32),
            jax.ShapeDtypeStruct((1, HID), F32),
            jax.ShapeDtypeStruct((HID, C), F32),
        ),
        in_specs=[vmem] * 10,
        out_specs=(vmem,) * 8,
        scratch_shapes=[
            pltpu.VMEM((TALL * WIDE, C), F32),
            pltpu.VMEM((TALL * WIDE, C), F32),
            pltpu.VMEM((KS, PAIRS, BS, 2 * C), BF16),
            pltpu.VMEM((KS, PAIRS, BS, 2 * C), BF16),
            pltpu.VMEM((KS * 4 * 2 * C, 2 * C), BF16),
            pltpu.VMEM((KS * 4 * 2 * C, 2 * C), BF16),
            pltpu.VMEM((2048, 2 * C), F32),
            pltpu.VMEM((2 * C, 2048), BF16),
            pltpu.VMEM((BS, BS, C), BF16),
            pltpu.VMEM((C + 16, HID), F32),
            pltpu.VMEM((C, HID), F32),
            pltpu.VMEM((3, 8, C), F32),
            pltpu.VMEM((2, 4, HALF, BS, C), BF16),
            pltpu.VMEM((2, 4, HALF, BS, C), BF16),
            pltpu.VMEM((2, 4, HALF, 16, C), BF16),
            pltpu.VMEM((n_lon * strip, C), F32),
            pltpu.VMEM((n_lon, strip, C), F32),
            pltpu.VMEM((n_lat, part, C), F32),
            pltpu.VMEM((strip, C), F32),
            pltpu.VMEM((n_lon, strip, C), F32),
            pltpu.VMEM((n_lon * small_part, C), F32),
            pltpu.VMEM((n_lon, small_part, C), F32),
            pltpu.VMEM((n_lat, small_part, C), F32),
            pltpu.VMEM((small_part, C), F32),
            pltpu.VMEM((n_lon, small_part, C), F32),
            pltpu.SemaphoreType.DMA((2, 8)),
            pltpu.SemaphoreType.DMA((2, 8)),
            pltpu.SemaphoreType.DMA((7, most)),
            pltpu.SemaphoreType.DMA((7, most)),
        ],
        compiler_params=pltpu.CompilerParams(
            collective_id=0, has_side_effects=True, vmem_limit_bytes=56 * 2**20
        ),
    )(
        cells, ocean_mask, cotangent, kernel, conv_bias[None, :], gain[None, :], shift[None, :],
        w_in, b_in[None, :], w_out,
    )
    g_cells, g_kernel, g_bias, g_gain, g_shift, g_in, g_b, g_out = outs
    return (g_cells, g_kernel, g_bias[0], g_gain[0], g_shift[0], g_in, g_b[0], g_out)


def solution(mesh):
    grid = P("lat", "lon", None)
    in_specs = (grid, P("lat", "lon"), grid) + (P(),) * 7
    out_specs = (grid,) + (P(),) * 7
    return jax.shard_map(
        functools.partial(body, mesh.shape["lon"], mesh.shape["lat"]),
        mesh=mesh, in_specs=in_specs, out_specs=out_specs, check_vma=False,
    )
```

time: 273 us -> 72.9 us (0.27)
  waiting for transfers between devices: 111 us -> 0 us
  other arithmetic: 70.9 us -> 0 us
  Pallas kernels: 0 us -> 64.8 us
  blocking collectives: 40.2 us -> 0 us
  matrix products: 18.3 us -> 0 us
  starting transfers between devices: 16 us -> 0 us
  between operations: 14.4 us -> 0.67 us
  local copies, waits for them, and re-layouts: 2.43 us -> 6.69 us
    psum x1 -> x0, waiting for transfers between devices: 98.5 us -> none  [body(): lax.psum((grad_kernel, grad_bias, grad_gain, grad_shift, grad_in, grad_b,...]
    pallas_call x0 -> x1, Pallas kernels: none -> 64.8 us  [body(): pl.pallas_call(functools.partial(block_kernel, n_lon, n_lat), out_shape=(...]
    reduce_sum x7 -> x0, other arithmetic: 43.4 us -> none  [the longest x4 21.2 us: section_two(): cols_list.append(jnp.sum(conv_wide * window, axis=(0, 1)))]
    psum x1 -> x0, blocking collectives: 40.2 us -> none  [body(): lax.psum((grad_kernel, grad_bias, grad_gain, grad_shift, grad_in, grad_b,...]
    convert_element_type x3 -> x0, other arithmetic: 18.7 us -> none  [the longest x1 16.7 us: body(): ((cotangent.astype(jnp.float32) + spread_back) * ocean.astype(jnp.float32...]
    dot_general x5 -> x0, matrix products: 18.3 us -> none  [the longest x1 6.66 us: section_one(): lax.dot_general(flat_grad, w_out, (((1,), (1,)), ((), ())), preferred_ele...]
    ppermute x8 -> x0, starting transfers between devices: 15.9 us -> none  [the longest x4 9.28 us: with_halo(): lax.ppermute(lax.slice_in_dim(block, block.shape[dim] - width, None, axis...]
    ppermute x8 -> x0, waiting for transfers between devices: 12.2 us -> none  [the longest x4 6.73 us: with_halo(): lax.ppermute(lax.slice_in_dim(block, block.shape[dim] - width, None, axis...]
  transfers between devices with their start and end apart: 9 -> 0, of which waited for: 7 -> 0; matrix products, arithmetic and copies ran while one was open for 7% -> 0% of each run, Pallas kernels for 0% -> 0%
where the time goes in v1:
time: 72.9 us; the launch traced here: 72.2 us
  Pallas kernels  64.8 us (89%)
  local copies, waits for them, and re-layouts  6.69 us (9%)
    pallas_call x1, Pallas kernels, body(): pl.pallas_call(functools.partial(block_kernel, n_lon, n_lat), out_shape=(...  64.8 us
    unnamed x22, local copies, waits for them, and re-layouts  6.69 us

profile of v1, /device:TPU:0, one launch (start us, length us, event | category | flops | bytes accessed | tf_op | source)
XLA Modules:
  0.0 72.2 jit_solution(9464593618682900283)
XLA Ops:
  0.6 64.8 %shard_map.161 = (bf16[64,64,128]{2,1,0:T(8,128)(2,1)}, f32[7,7,128]{2,1,0:T(8,128)}, f32[1,128]{1,0:T(1,128)}, f32[1,128]{1,0:T(1,128)}, f32[1,128]{1,0:T(1,128...) custom-call(bf16[64,64,128]{2,1,0:T(8,128)(2,1)} %cells.1, s32[64,64]{1,0:T(8,128)} %mask.1, ...), custom_call_target="tpu_custom_call" | custom-call | tf_op jit(solution)/shard_map/pallas_call | solution.py:386
  65.5 0.0 copy-start.2
  65.5 0.0 copy-start.1
  65.5 2.3 %copy.26 = bf16[64,64,128]{2,1,0:T(8,128)(2,1)} copy(bf16[64,64,128]{2,1,0:T(8,128)(2,1)} %get-tuple-element.32) | data formatting | bytes 2097152
  67.8 0.0 copy-done.2
  67.8 0.0 copy-start.6
  67.8 0.6 copy.27
  68.4 0.0 copy-done.6
  68.4 0.0 copy-start.5
  68.4 0.5 copy.28
  68.9 0.1 copy-done.5
  69.0 0.0 copy-start.4
  69.0 0.5 copy.29
  69.5 0.1 copy-done.4
  69.7 0.5 copy.30
  70.2 0.0 copy-done.1
  70.2 0.0 copy-start.3
  70.2 0.0 copy-start
  70.2 0.7 copy.31
  70.9 0.0 copy-done.3
  70.9 0.6 copy.32
  71.5 0.0 copy-done
  71.5 0.7 copy.33
Async XLA Ops:
  65.5 2.3 %copy-start.2 = (f32[7,7,128]{2,1,0:T(8,128)S(1)}, f32[7,7,128]{2,1,0:T(8,128)}, u32[]{:S(2)}) copy-start(f32[7,7,128]{2,1,0:T(8,128)} %get-tuple-element.33) | copy-start | bytes 75268
  65.5 4.7 %copy-start.1 = (f32[128,512]{1,0:T(8,128)S(1)}, f32[128,512]{1,0:T(8,128)}, u32[]{:S(2)}) copy-start(f32[128,512]{1,0:T(8,128)} %get-tuple-element.37) | copy-start | bytes 786436
  67.8 0.6 copy-start.6
  68.4 0.6 copy-start.5
  69.0 0.6 copy-start.4
  70.2 0.7 copy-start.3
  70.2 1.3 %copy-start = (f32[512,128]{1,0:T(8,128)S(1)}, f32[512,128]{1,0:T(8,128)}, u32[]{:S(2)}) copy-start(f32[512,128]{1,0:T(8,128)} %get-tuple-element.39) | copy-start | bytes 786436

commit v2 on v1

--- a/solution.py
+++ b/solution.py
@@ -178,16 +178,22 @@
     halo_wait(0, padf, padf3)
     spread_pairs(padf3, padp)
 
-    def forward(t, carry):
-        convb[pl.ds(t * 512, 512), :] = conv_chunk(padp, w_fwd, t)
-        return carry
-    lax.fori_loop(0, 4, forward, 0)
+    def conv_piece(t, first, last):
+        taps = [
+            padp[b, pl.ds(8 * t + q, 8)].reshape(8 * BS, 2 * C)
+            for b in range(first, last) for q in range(4)
+        ]
+        out = mm(jnp.concatenate(taps, axis=1), w_fwd[first * 8 * C : last * 8 * C, :])
+        rows = pl.ds(pl.multiple_of(t * 512, 512), 512)
+        convb[rows, :] = out if first == 0 else convb[rows, :] + out
+
+    conv_piece(0, 0, KS)
 
     c1 = math.sqrt(2.0 / math.pi)
     c2 = c1 * 0.044715
     order = (0, 2, 4, 6, 1, 3, 5, 7)
 
-    def cell_chunk(t, carry):
+    def cell_chunk(t, beside=(None, None)):
         two = convb[pl.ds(pl.multiple_of(t * 256, 256), 256), :]
         conv = jnp.concatenate([two[:, :C], two[:, C:]], axis=0) + bias[...]
         centred = conv - jnp.mean(conv, axis=-1, keepdims=True)
@@ -201,6 +207,8 @@
         left = jnp.concatenate([normed_t, ones], axis=0)
         norm_grad = jnp.zeros((512, C), F32)
         for h in range(2):
+            if beside[h] is not None:
+                beside[h]()
             cols = slice(h * 256, (h + 1) * 256)
             v = mm(normed, w_in[:, cols]) + b_in[:, cols]
             act_grad = mm(og, w_out[cols, :], ((1,), (1,)))
@@ -229,8 +237,18 @@
         ).T
         for n, i in enumerate(order):
             gradf3[HALF + 8 * t + i, LEFT : LEFT + BS, :] = wide[n * BS : (n + 1) * BS]
+
+    def two_chunks(t, carry):
+        piece = functools.partial(conv_piece, t + 1)
+        cell_chunk(2 * t, (lambda: piece(0, 2), lambda: piece(2, 4)))
+        cell_chunk(2 * t + 1, (lambda: piece(4, 6), lambda: piece(6, 7)))
         return carry
-    lax.fori_loop(0, 8, cell_chunk, 0)
+    lax.fori_loop(0, 3, two_chunks, 0)
+
+    def last_chunk(t, carry):
+        cell_chunk(t)
+        return carry
+    lax.fori_loop(6, 8, last_chunk, 0)
 
     halo_send(1, gradf, gradf3)
 
@@ -302,6 +320,13 @@
     )
     send_parts(small, small_part, small_lon, 1)
 
+    end(big, strip, big_lon, 0, lons, "lon")
+    big_sum[...] = total(big_lon, n_lon)
+    for other in lats:
+        at = pl.multiple_of(other * part, 8)
+        copy(big_sum.at[pl.ds(at, part)], big_lat, 2, lat, other, dev(other, lon)).start()
+    big_lat[lat] = big_sum[pl.ds(pl.multiple_of(lat * part, 8), part), :]
+
     halo_wait(1, gradf, gradf3)
     spread_pairs(gradf3, gradp)
 
@@ -313,25 +338,8 @@
                 back = two[i * BS : (i + 1) * BS, e * C : (e + 1) * C]
                 o_cells[row] = ((cot[row].astype(F32) + back) * maskx[row].astype(F32)).astype(BF16)
 
-    backward(0)
-    end(big, strip, big_lon, 0, lons, "lon")
-    end(small, small_part, small_lon, 1, lons, "lon")
-    big_sum[...] = total(big_lon, n_lon)
-    small_sum[...] = total(small_lon, n_lon)
-    for other in lats:
-        at = pl.multiple_of(other * part, 8)
-        copy(big_sum.at[pl.ds(at, part)], big_lat, 2, lat, other, dev(other, lon)).start()
-        copy(small_sum, small_lat, 3, lat, other, dev(other, lon)).start()
-    big_lat[lat] = big_sum[pl.ds(pl.multiple_of(lat * part, 8), part), :]
-    small_lat[lat] = small_sum[...]
-
-    backward(1)
-    end(big_sum, part, big_lat, 2, lats, "lat")
-    end(small_sum, small_part, small_lat, 3, lats, "lat")
     factor = 1.0 / math.sqrt(float(BS * BS * n_lon * n_lat))
     own = pl.ds(pl.multiple_of(lat * part, 8), part)
-    big_all[lon, own, :] = total(big_lat, n_lat) * factor
-    small_all[lon] = total(small_lat, n_lat) * factor
 
     def spread_lat(other):
         return pltpu.make_async_remote_copy(
@@ -340,12 +348,17 @@
             device_id=dev(other, lon), device_id_type=MESH,
         )
 
+    end(big_sum, part, big_lat, 2, lats, "lat")
+    big_all[lon, own, :] = total(big_lat, n_lat) * factor
     for other in lats:
         spread_lat(other).start()
-    for other in lons:
-        copy(small_all.at[lon], small_all, 6, lon, other, dev(lat, other)).start()
-
-    backward(2)
+    end(small, small_part, small_lon, 1, lons, "lon")
+    small_sum[...] = total(small_lon, n_lon)
+    for other in lats:
+        copy(small_sum, small_lat, 3, lat, other, dev(other, lon)).start()
+    small_lat[lat] = small_sum[...]
+
+    backward(0)
     for other in lats:
         spread_lat(other).wait_send()
         theirs = big_all.at[lon, pl.ds(pl.multiple_of(other * part, 8), part)]
@@ -355,7 +368,13 @@
         ).wait_recv()
     for other in lons:
         copy(big_all.at[lon], big_all, 5, lon, other, dev(lat, other)).start()
-
+    end(small_sum, small_part, small_lat, 3, lats, "lat")
+    small_all[lon] = total(small_lat, n_lat) * factor
+    for other in lons:
+        copy(small_all.at[lon], small_all, 6, lon, other, dev(lat, other)).start()
+
+    backward(1)
+    backward(2)
     backward(3)
     for other in lons:
         copy(big_all.at[lon], big_all, 5, lon, other, dev(lat, other)).wait_send()
@@ -376,6 +395,14 @@
     o_shift[...] = rest[58:59, :]
     for h in range(4):
         o_b[:, h * C : (h + 1) * C] = rest[59 + h : 60 + h, :]
+
+
+def hand_out(*refs):
+    copies = [pltpu.make_async_copy(refs[k], refs[8 + k], refs[16].at[k]) for k in range(8)]
+    for each in copies:
+        each.start()
+    for each in copies:
+        each.wait()
 
 
 def body(n_lon, n_lat, cells, ocean_mask, cotangent, kernel, conv_bias, gain, shift, w_in, b_in, w_out):
@@ -435,6 +462,14 @@
         cells, ocean_mask, cotangent, kernel, conv_bias[None, :], gain[None, :], shift[None, :],
         w_in, b_in[None, :], w_out,
     )
+    anywhere = pl.BlockSpec(memory_space=pl.ANY)
+    outs = pl.pallas_call(
+        hand_out,
+        out_shape=tuple(jax.ShapeDtypeStruct(x.shape, x.dtype) for x in outs),
+        in_specs=[anywhere] * 8,
+        out_specs=(anywhere,) * 8,
+        scratch_shapes=[pltpu.SemaphoreType.DMA((8,))],
+    )(*outs)
     g_cells, g_kernel, g_bias, g_gain, g_shift, g_in, g_b, g_out = outs
     return (g_cells, g_kernel, g_bias[0], g_gain[0], g_shift[0], g_in, g_b[0], g_out)
 

time: 72.9 us -> 109 us (1.50)
  Pallas kernels: 64.8 us -> 108 us
  local copies, waits for them, and re-layouts: 6.69 us -> 0 us
    pallas_call x0 -> x1, Pallas kernels: none -> 49.7 us  [body(): pl.pallas_call(hand_out, out_shape=tuple((jax.ShapeDtypeStruct(x.shape, x...]
    unnamed x22 -> x0, local copies, waits for them, and re-layouts: 6.69 us -> none
    pallas_call x1, Pallas kernels: 64.8 us -> 58.8 us  [body(): pl.pallas_call(functools.partial(block_kernel, n_lon, n_lat), out_shape=(...]
where the time goes in v2:
time: 109 us
  Pallas kernels  108 us (99%)
    pallas_call x1, Pallas kernels, body(): pl.pallas_call(functools.partial(block_kernel, n_lon, n_lat), out_shape=(...  58.8 us
    pallas_call x1, Pallas kernels, body(): pl.pallas_call(hand_out, out_shape=tuple((jax.ShapeDtypeStruct(x.shape, x...  49.7 us

profile of v2, /device:TPU:0, one launch (start us, length us, event | category | flops | bytes accessed | tf_op | source)
XLA Modules:
  0.0 109.3 jit_solution(17864977864664909456)
XLA Ops:
  0.6 58.8 %shard_map.161 = (bf16[64,64,128]{2,1,0:T(8,128)(2,1)}, f32[7,7,128]{2,1,0:T(8,128)}, f32[1,128]{1,0:T(1,128)}, f32[1,128]{1,0:T(1,128)}, f32[1,128]{1,0:T(1,128...) custom-call(bf16[64,64,128]{2,1,0:T(8,128)(2,1)} %cells.1, s32[64,64]{1,0:T(8,128)} %mask.1, ...), custom_call_target="tpu_custom_call" | custom-call | tf_op jit(solution)/shard_map/pallas_call | solution.py:413
  59.4 49.7 %shard_map.162 = (bf16[64,64,128]{2,1,0:T(8,128)(2,1)}, f32[7,7,128]{2,1,0:T(8,128)}, f32[1,128]{1,0:T(1,128)}, f32[1,128]{1,0:T(1,128)}, f32[1,128]{1,0:T(1,128...) custom-call(bf16[64,64,128]{2,1,0:T(8,128)(2,1)} %get-tuple-element.24.refs_0_, ...), custom_call_target="tpu_custom_call" | custom-call | tf_op jit(solution)/shard_map/pallas_call | solution.py:466

commit v3 on v2

--- a/solution.py
+++ b/solution.py
@@ -398,11 +398,8 @@
 
 
 def hand_out(*refs):
-    copies = [pltpu.make_async_copy(refs[k], refs[8 + k], refs[16].at[k]) for k in range(8)]
-    for each in copies:
-        each.start()
-    for each in copies:
-        each.wait()
+    for k in range(8):
+        refs[8 + k][...] = refs[k][...]
 
 
 def body(n_lon, n_lat, cells, ocean_mask, cotangent, kernel, conv_bias, gain, shift, w_in, b_in, w_out):
@@ -462,13 +459,11 @@
         cells, ocean_mask, cotangent, kernel, conv_bias[None, :], gain[None, :], shift[None, :],
         w_in, b_in[None, :], w_out,
     )
-    anywhere = pl.BlockSpec(memory_space=pl.ANY)
     outs = pl.pallas_call(
         hand_out,
         out_shape=tuple(jax.ShapeDtypeStruct(x.shape, x.dtype) for x in outs),
-        in_specs=[anywhere] * 8,
-        out_specs=(anywhere,) * 8,
-        scratch_shapes=[pltpu.SemaphoreType.DMA((8,))],
+        in_specs=[vmem] * 8,
+        out_specs=(vmem,) * 8,
     )(*outs)
     g_cells, g_kernel, g_bias, g_gain, g_shift, g_in, g_b, g_out = outs
     return (g_cells, g_kernel, g_bias[0], g_gain[0], g_shift[0], g_in, g_b[0], g_out)

time: 109 us -> 62.2 us (0.57)
  Pallas kernels: 108 us -> 61.3 us
    pallas_call x1, Pallas kernels: 49.7 us -> 2.55 us  [body(): pl.pallas_call(hand_out, out_shape=tuple((jax.ShapeDtypeStruct(x.shape, x...]
where the time goes in v3:
time: 62.2 us; the launch traced here: 62 us
  Pallas kernels  61.3 us (99%)
  between operations  0.72 us (1%)
    pallas_call x1, Pallas kernels, body(): pl.pallas_call(functools.partial(block_kernel, n_lon, n_lat), out_shape=(...  58.8 us
    pallas_call x1, Pallas kernels, body(): pl.pallas_call(hand_out, out_shape=tuple((jax.ShapeDtypeStruct(x.shape, x...  2.55 us

profile of v3, /device:TPU:0, one launch (start us, length us, event | category | flops | bytes accessed | tf_op | source)
XLA Modules:
  0.0 62.0 jit_solution(14288443118579437665)
XLA Ops:
  0.6 58.8 %shard_map.161 = (bf16[64,64,128]{2,1,0:T(8,128)(2,1)}, f32[7,7,128]{2,1,0:T(8,128)}, f32[1,128]{1,0:T(1,128)}, f32[1,128]{1,0:T(1,128)}, f32[1,128]{1,0:T(1,128...) custom-call(bf16[64,64,128]{2,1,0:T(8,128)(2,1)} %cells.1, s32[64,64]{1,0:T(8,128)} %mask.1, ...), custom_call_target="tpu_custom_call" | custom-call | tf_op jit(solution)/shard_map/pallas_call | solution.py:410
  59.4 2.6 %shard_map.162 = (bf16[64,64,128]{2,1,0:T(8,128)(2,1)}, f32[7,7,128]{2,1,0:T(8,128)}, f32[1,128]{1,0:T(1,128)}, f32[1,128]{1,0:T(1,128)}, f32[1,128]{1,0:T(1,128...) custom-call(bf16[64,64,128]{2,1,0:T(8,128)(2,1)} %get-tuple-element.24.refs_0_, ...), custom_call_target="tpu_custom_call" | custom-call | tf_op jit(solution)/shard_map/pallas_call | solution.py:462
